TPU v7x, 256 devices: a whole 4x4x8 slice. The times are simulated.
256 devices in a mesh: dp: 32 (over z, y_hi, core), tensor: 8 (over x, y_lo).
Axes of the slice: x: 4, y: 4 (y_hi: 2, y_lo: 2; y = y_hi * 2 + y_lo), z: 8, core: 2. Of those that a mesh axis runs over, the one named last changes fastest.
Arguments:
- inputs: bfloat16 [2048, 8192], P('tensor', 'dp'), may hold values from -6 to 6
- gate_pre: bfloat16 [2048, 14336], P('dp', 'tensor'), may hold values from -8 to 8
- up_pre: bfloat16 [2048, 14336], P('dp', 'tensor'), may hold values from -6 to 6
- hidden_grad: bfloat16 [2048, 14336], P('dp', 'tensor'), may hold values from -6 to 6
- gate_weight: bfloat16 [8192, 14336], P('dp', 'tensor'), may hold values from -0.046875 to 0.046875
- up_weight: bfloat16 [8192, 14336], P('dp', 'tensor'), may hold values from -0.046875 to 0.046875
Outputs:
- input_grad: bfloat16 [2048, 8192], P('tensor', 'dp')
- gate_wgrad: float32 [8192, 14336], P('dp', 'tensor')
- up_wgrad: float32 [8192, 14336], P('dp', 'tensor')
All inputs are finite; a program needn't handle non-finite values.
Results may differ from a plain program's by a relative error of at most 0.017.
Values may be sent and summed in bfloat16 or wider, within the bound.
A program may use at most 64 MiB of HBM per device.

v0:
```python
import math

import jax
import jax.numpy as jnp
from jax import lax
from jax.sharding import PartitionSpec as P


def row_product(left_rows, right_rows):
    return lax.dot_general(
        left_rows, right_rows, (((0,), (0,)), ((), ())), preferred_element_type=jnp.float32
    )


def feature_product(grad_rows, weight_tile):
    return lax.dot_general(
        grad_rows, weight_tile, (((1,), (1,)), ((), ())), preferred_element_type=jnp.float32
    )


def per_device(inputs, gate_pre, up_pre, hidden_grad, gate_weight, up_weight):
    gate_value = gate_pre.astype(jnp.float32)
    up_value = up_pre.astype(jnp.float32)
    grad_value = hidden_grad.astype(jnp.float32)
    sigmoid_gate = 1.0 / (1.0 + jnp.exp(-gate_value))
    up_grad = (grad_value * gate_value * sigmoid_gate).astype(jnp.bfloat16)
    gate_grad = (
        grad_value * up_value * sigmoid_gate * (1.0 + gate_value * (1.0 - sigmoid_gate))
    ).astype(jnp.bfloat16)
    all_inputs = lax.all_gather(inputs, "tensor", axis=0, tiled=True)
    row_total = all_inputs.shape[0]
    grad_scale = 1.0 / math.sqrt(row_total)
    gate_all, up_all = (
        lax.all_gather(gate_grad, "dp", axis=0, tiled=True),
        lax.all_gather(up_grad, "dp", axis=0, tiled=True),
    )
    gate_total = row_product(all_inputs, gate_all)
    up_total = row_product(all_inputs, up_all)
    gate_wgrad = gate_total * grad_scale
    up_wgrad = up_total * grad_scale
    partial_terms = feature_product(gate_all, gate_weight) + feature_product(up_all, up_weight)
    input_grad = lax.psum_scatter(
        partial_terms.astype(jnp.bfloat16), "tensor", scatter_dimension=0, tiled=True
    )
    return (input_grad, gate_wgrad, up_wgrad)


def solution(mesh):
    in_specs = (
        P("tensor", "dp"),
        P("dp", "tensor"),
        P("dp", "tensor"),
        P("dp", "tensor"),
        P("dp", "tensor"),
        P("dp", "tensor"),
    )
    out_specs = (P("tensor", "dp"), P("dp", "tensor"), P("dp", "tensor"))
    return jax.shard_map(
        per_device, mesh=mesh, in_specs=in_specs, out_specs=out_specs, check_vma=False
    )
```

profile of v0, /device:TPU:20, one launch (start us, length us, event | category | flops | bytes accessed | tf_op | source)
XLA Modules:
  0.0 297.8 jit_solution(4170685655298111625)
XLA Ops:
  7.2 0.0 copy-start
  7.2 0.0 all-gather.4.cloned.1.call-start
  7.2 2.2 fusion.11
  9.5 0.0 all-gather.4.cloned.1.call-update
  9.5 0.0 all-gather.6.cloned.1.call-start
  9.5 0.7 all-gather.6.cloned.1.call-update
  10.2 0.0 all-gather.8.cloned.1.call-start
  10.3 0.7 all-gather.8.cloned.1.call-update
  11.0 0.0 copy-start.1
  11.0 0.0 reduce-scatter.2.cloned.1.call-start
  11.0 98.5 %all-gather.4.cloned.1.call-done = bf16[2048,1792]{1,0:T(8,128)(2,1)} async-done(((bf16[64,1792]{1,0:T(8,128)(2,1)}), bf16[2048,1792]{1,0:T(8,128)(2,1)}) %all-gather.4.cloned.1.call-update) | async-done | bytes 7340048 | tf_op jit(solution)/shard_map/all_gather | solution.py:34
  109.5 0.0 copy-done
  109.5 6.5 %fusion.12 = f32[2048,256]{1,0:T(8,128)} fusion(bf16[2048,1792]{1,0:T(8,128)(2,1)} %all-gather.4.cloned.1.call-done, bf16[256,1792]{1,0:T(8,128)(2,1)S(1)} %copy-done), kind=kOutput, calls=%fused_computation.19 | convolution fusion | flops 1879048192 | bytes 10354688 | tf_op jit(solution)/shard_map/dot_general | solution.py:16
  116.0 91.4 %all-gather.6.cloned.1.call-done = bf16[2048,1792]{1,0:T(8,128)(2,1)} async-done(((bf16[64,1792]{1,0:T(8,128)(2,1)}), bf16[2048,1792]{1,0:T(8,128)(2,1)}) %all-gather.6.cloned.1.call-update) | async-done | bytes 7340048 | tf_op jit(solution)/shard_map/all_gather | solution.py:35
  207.4 0.0 copy-done.1
  207.4 6.8 %fusion.2 = bf16[2048,256]{1,0:T(8,128)(2,1)} fusion(f32[2048,256]{1,0:T(8,128)} %fusion.12, bf16[2048,1792]{1,0:T(8,128)(2,1)} %all-gather.6.cloned.1.call-done, bf16[256,1792]{1,0:T(8,128)(2,1)S(1)} %copy-done.1), kind=kOutput, calls=%fused_computation.5 | convolution fusion | flops 1880096768 | bytes 11403264 | tf_op jit(solution)/shard_map/dot_general | solution.py:16
  214.2 0.0 reduce-scatter.2.cloned.1.call-update
  214.2 33.3 %all-gather.8.cloned.1.call-done = bf16[2048,256]{1,0:T(8,128)(2,1)} async-done(((bf16[256,256]{1,0:T(8,128)(2,1)}), bf16[2048,256]{1,0:T(8,128)(2,1)}) %all-gather.8.cloned.1.call-update) | async-done | bytes 1048592 | tf_op jit(solution)/shard_map/all_gather | solution.py:30
  247.6 5.4 %fusion.1 = f32[256,1792]{0,1:T(8,128)S(1)} fusion(bf16[2048,1792]{1,0:T(8,128)(2,1)} %all-gather.6.cloned.1.call-done, bf16[2048,256]{1,0:T(8,128)(2,1)} %all-gather.8.cloned.1.call-done), kind=kOutput, calls=%fused_computation.3 | convolution fusion | flops 1879506944 | bytes 10223616 | tf_op jit(solution)/shard_map/dot_general | solution.py:10
  253.0 1.7 copy.10
  254.7 5.4 %fusion = f32[256,1792]{0,1:T(8,128)S(1)} fusion(bf16[2048,1792]{1,0:T(8,128)(2,1)} %all-gather.4.cloned.1.call-done, bf16[2048,256]{1,0:T(8,128)(2,1)} %all-gather.8.cloned.1.call-done), kind=kOutput, calls=%fused_computation.2 | convolution fusion | flops 1879506944 | bytes 10223616 | tf_op jit(solution)/shard_map/dot_general | solution.py:10
  260.1 1.7 copy.9
  261.8 29.5 %reduce-scatter.2.cloned.1.call-done = bf16[256,256]{1,0:T(8,128)(2,1)} async-done(((bf16[2048,256]{1,0:T(8,128)(2,1)}), bf16[256,256]{1,0:T(8,128)(2,1)}) %reduce-scatter.2.cloned.1.call-update) | async-done | bytes 131088 | tf_op jit(solution)/shard_map/reduce_scatter | solution.py:42
Async XLA Ops:
  7.2 102.4 %copy-start = (bf16[256,1792]{1,0:T(8,128)(2,1)S(1)}, bf16[256,1792]{1,0:T(8,128)(2,1)}, u32[]{:S(2)}) copy-start(bf16[256,1792]{1,0:T(8,128)(2,1)} %param.10) | copy-start | bytes 2752516
  7.2 102.4 %all-gather.4.cloned.1.call-start = ((), (), s32[]{:S(2)}) async-start(), calls=%async_computation.1 | async-start | bytes 7569408 | tf_op jit(solution)/shard_map/all_gather | solution.py:34
  9.5 197.9 %all-gather.6.cloned.1.call-start = ((), (), s32[]{:S(2)}) async-start(), calls=%async_computation.2 | async-start | bytes 7569408 | tf_op jit(solution)/shard_map/all_gather | solution.py:35
  10.2 237.3 %all-gather.8.cloned.1.call-start = ((), (), s32[]{:S(2)}) async-start(), calls=%async_computation.4 | async-start | bytes 1179648 | tf_op jit(solution)/shard_map/all_gather | solution.py:30
  11.0 196.4 %copy-start.1 = (bf16[256,1792]{1,0:T(8,128)(2,1)S(1)}, bf16[256,1792]{1,0:T(8,128)(2,1)}, u32[]{:S(2)}) copy-start(bf16[256,1792]{1,0:T(8,128)(2,1)} %param.11) | copy-start | bytes 2752516
  11.0 280.3 %reduce-scatter.2.cloned.1.call-start = ((), (), s32[]{:S(2)}) async-start(), calls=%async_computation.3 | async-start | bytes 1179648 | tf_op jit(solution)/shard_map/reduce_scatter | solution.py:42
Sparse Core Ops, SparseCore 0:
  11.4 98.1 all-gather.3
  112.9 94.4 all-gather.5
  209.2 38.3 all-gather.7
  250.5 40.7 reduce-scatter.1
where the time goes:
time: 301 us; the launch traced here: 298 us
  waiting for transfers between devices  254 us (84%)
  matrix products  24.1 us (8%)
  between operations  13.8 us (5%)
  local copies, waits for them, and re-layouts  3.39 us (1%)
    all_gather x1, waiting for transfers between devices, per_device(): lax.all_gather(gate_grad, 'dp', axis=0, tiled=True)  98.5 us
    all_gather x1, waiting for transfers between devices, per_device(): lax.all_gather(up_grad, 'dp', axis=0, tiled=True)  91.4 us
    all_gather x1, waiting for transfers between devices, per_device(): all_inputs = lax.all_gather(inputs, 'tensor', axis=0, tiled=True)  33.3 us
    reduce_scatter x1, waiting for transfers between devices, per_device(): lax.psum_scatter(partial_terms.astype(jnp.bfloat16), 'tensor', scatter_di...  29.5 us
    dot_general x2, matrix products, feature_product(): lax.dot_general(grad_rows, weight_tile, (((1,), (1,)), ((), ())), preferr...  13.3 us
    dot_general x2, matrix products, row_product(): lax.dot_general(left_rows, right_rows, (((0,), (0,)), ((), ())), preferre...  10.8 us
  transfers between devices with their start and end apart: 4, of which 4 were waited for; matrix products, arithmetic and copies ran while one was open for 9% of the time, Pallas kernels for 0%

commit v1 on v0

v1 whole, which is shorter than its diff:
```python
import functools
import math

import jax
import jax.numpy as jnp
from jax import lax
from jax.experimental import pallas as pl
from jax.experimental.pallas import tpu as pltpu
from jax.sharding import PartitionSpec as P

MESH = pl.DeviceIdType.MESH
ROWS = 64
GROUP = 256
HID = 1792
FEAT = 256
NZ = 8
NX = 4
GATE, UP = 0, 1
SCALE = 1.0 / math.sqrt(2048)
OFFS = (0, -1, 1, -2, 2, -3, 3, 4)


def kernel(
    inputs, gate_pre, up_pre, hidden_grad, gate_weight, up_weight,
    igrad_out, gate_out, up_out,
    grads, xs, xt, w, wt, acc, part, part_b, rx, ry, sy, fin, pre,
    loc, z_s, z_r, f_s, f_r, y_s, y_r, c_s, c_r, x_s, x_r, g_s, g_r, h_s, h_r, out_sem,
):
    dp, tensor = lax.axis_index("dp"), lax.axis_index("tensor")
    z, yh, c = dp // 4, (dp // 2) % 2, dp % 2
    x, yl = tensor // 2, tensor % 2

    def at_z(step):
        return {"dp": ((z + step + NZ) % NZ) * 4 + yh * 2 + c, "tensor": tensor}

    opposite = {"dp": z * 4 + (1 - yh) * 2 + c, "tensor": tensor}
    sibling = {"dp": z * 4 + yh * 2 + (1 - c), "tensor": tensor}
    partner = {"dp": dp, "tensor": x * 2 + (1 - yl)}

    def at_x(step):
        return {"dp": dp, "tensor": ((x + step) % NX) * 2 + yl}

    def group(off):
        return (z + off + NZ) % NZ

    own_rows = pl.multiple_of(yh * 128 + c * ROWS, ROWS)
    opp_rows = pl.multiple_of((1 - yh) * 128 + c * ROWS, ROWS)

    def block(kind, src_z, far):
        return grads.at[kind, src_z, pl.ds(opp_rows if far else own_rows, ROWS), :]

    def remote(src, dst, s, r, dev):
        return pltpu.make_async_remote_copy(
            src_ref=src, dst_ref=dst, send_sem=s, recv_sem=r, device_id=dev, device_id_type=MESH
        )

    STREAM = ((GATE, 0), (UP, 0), (UP, 1))

    def z_copy(way, stream, hop):
        kind, far = STREAM[stream]
        step = 1 - 2 * way
        b = block(kind, group(-step * hop), far)
        return remote(b, b, z_s.at[way, stream, hop], z_r.at[way, stream, hop], at_z(step))

    def far_copy(stream):
        kind, far = STREAM[stream]
        step = 1 - 2 * c
        b = block(kind, group(-3 * step), far)
        return remote(b, b, f_s.at[stream], f_r.at[stream], at_z(step))

    def y_copy(kind, off):
        slot = NZ if kind == UP else off % NZ
        b = block(kind, group(off), 0)
        return remote(b, b, y_s.at[slot], y_r.at[slot], opposite)

    def c_copy(kind, far, off):
        b = block(kind, group(off), far)
        i = off % NZ
        return remote(b, b, c_s.at[kind, far, i], c_r.at[kind, far, i], sibling)

    def x_copy(slot):
        if slot == 0:
            return remote(inputs, xs.at[tensor], x_s.at[0], x_r.at[0], partner)
        if slot <= 3:
            return remote(inputs, xs.at[tensor], x_s.at[slot], x_r.at[slot], at_x(slot))
        b = xs.at[x * 2 + (1 - yl)]
        return remote(b, b, x_s.at[slot], x_r.at[slot], at_x(slot - 3))

    pre_loads = [
        pltpu.make_async_copy(ref, pre.at[i], loc.at[i])
        for i, ref in enumerate((gate_pre, up_pre, hidden_grad))
    ]
    w_loads = [
        pltpu.make_async_copy(ref, w.at[i], loc.at[3 + i])
        for i, ref in enumerate((gate_weight, up_weight))
    ]
    x_load = pltpu.make_async_copy(inputs, xs.at[tensor], loc.at[5])
    for cp in pre_loads + w_loads + [x_load]:
        cp.start()

    barrier = pltpu.get_barrier_semaphore()
    peers = [at_z(1), at_z(-1), opposite, sibling, partner, at_x(1), at_x(2), at_x(3)]
    for peer in peers:
        pl.semaphore_signal(barrier, inc=1, device_id=peer, device_id_type=MESH)

    for cp in pre_loads:
        cp.wait()

    def elementwise(i, _):
        cols = pl.ds(pl.multiple_of(i * 256, 256), 256)
        gate_value = pre[0, :, cols].astype(jnp.float32)
        up_value = pre[1, :, cols].astype(jnp.float32)
        grad_value = pre[2, :, cols].astype(jnp.float32)
        sig = 1.0 / (1.0 + jnp.exp(-gate_value))
        grads[UP, z, pl.ds(own_rows, ROWS), cols] = (grad_value * gate_value * sig).astype(jnp.bfloat16)
        grads[GATE, z, pl.ds(own_rows, ROWS), cols] = (
            grad_value * up_value * sig * (1.0 + gate_value * (1.0 - sig))
        ).astype(jnp.bfloat16)
        return 0

    lax.fori_loop(0, HID // 256, elementwise, 0)
    pl.semaphore_wait(barrier, len(peers))

    started = []

    def go(cp):
        cp.start()
        started.append(cp)

    def arrive_z(stream, hop):
        kind, far = STREAM[stream]
        for way in (0, 1):
            z_copy(way, stream, hop).wait_recv()
            if hop < 2:
                go(z_copy(way, stream, hop + 1))
        if hop == 2:
            go(far_copy(stream))
        for off in (-(hop + 1), hop + 1):
            if kind == GATE:
                go(y_copy(GATE, off))
            go(c_copy(kind, far, off))

    def arrive_far(stream):
        kind, far = STREAM[stream]
        far_copy(stream).wait_recv()
        if kind == GATE:
            go(y_copy(GATE, 4))
        go(c_copy(kind, far, 4))

    def arrive_y(off):
        y_copy(GATE, off).wait_recv()
        go(c_copy(GATE, 1, off))

    def from_sibling(kind, off):
        for far in (0, 1):
            c_copy(kind, far, off).wait_recv()

    def wgrad(kind, off):
        g = group(off)
        for half in (0, 1):
            cols = pl.ds(half * 896, 896)
            prod = jnp.dot(xt[g], grads[kind, g, :, cols], preferred_element_type=jnp.float32)
            if off != 0:
                prod = acc[kind, :, cols] + prod
            if off == 4:
                prod = prod * SCALE
            acc[kind, :, cols] = prod

    def igrad(kind, off):
        g = group(off)
        prod = jnp.dot(grads[kind, g], wt[kind], preferred_element_type=jnp.float32)
        if kind == GATE:
            part[g] = prod
        else:
            part_b[g] = (part[g] + prod).astype(jnp.bfloat16)

    def scatter(off):
        g = group(off)
        gx, gl = g // 2, g % 2
        i = off % NZ
        slot = (x - gx + NX) % NX - 1

        def copy():
            return remote(
                part_b.at[g], rx.at[gl, slot], g_s.at[i], g_r.at[gl, slot],
                {"dp": dp, "tensor": gx * 2 + yl},
            )

        return x != gx, copy

    def send_part(off):
        cond, copy = scatter(off)
        pl.when(cond)(lambda: copy().start())

    for way in (0, 1):
        go(z_copy(way, 0, 0))
    go(y_copy(UP, 0))
    for way in (0, 1):
        go(z_copy(way, 1, 0))
    go(c_copy(UP, 0, 0))
    go(c_copy(GATE, 0, 0))
    go(x_copy(0))
    go(y_copy(GATE, 0))
    for slot in (1, 2, 3):
        go(x_copy(slot))

    for cp in w_loads:
        cp.wait()

    def flip_w(i, _):
        cols = pl.ds(pl.multiple_of(i * 256, 256), 256)
        for kind in (GATE, UP):
            wt[kind, cols, :] = w[kind, :, cols].T
        return 0

    x_copy(0).wait_recv()
    for slot in (4, 5, 6):
        go(x_copy(slot))
    lax.fori_loop(0, HID // 256, flip_w, 0)

    arrive_z(0, 0)
    y_copy(UP, 0).wait_recv()
    for way in (0, 1):
        go(z_copy(way, 2, 0))
    go(c_copy(UP, 1, 0))
    arrive_z(1, 0)
    arrive_y(0)

    x_load.wait()
    for slot in range(1, 7):
        x_copy(slot).wait_recv()

    def flip_x(i, _):
        xt[i] = xs[i].T
        return 0

    lax.fori_loop(0, NZ, flip_x, 0)

    def do(kind, off):
        from_sibling(kind, off)
        igrad(kind, off)
        if kind == UP:
            send_part(off)
        wgrad(kind, off)

    do(GATE, 0)
    do(UP, 0)
    arrive_z(0, 1)
    arrive_y(-1)
    arrive_z(2, 0)
    arrive_y(1)
    do(GATE, -1)
    do(GATE, 1)
    arrive_z(1, 1)
    arrive_y(-2)
    do(UP, -1)
    do(UP, 1)
    arrive_z(0, 2)
    arrive_y(2)
    do(GATE, -2)
    do(GATE, 2)
    arrive_z(2, 1)
    arrive_y(-3)
    do(UP, -2)
    do(UP, 2)
    arrive_z(1, 2)
    arrive_y(3)
    do(GATE, -3)
    do(GATE, 3)
    arrive_far(0)
    arrive_z(2, 2)
    do(UP, -3)
    do(UP, 3)
    arrive_far(1)
    arrive_y(4)
    do(GATE, 4)
    gate_store = pltpu.make_async_copy(acc.at[GATE], gate_out, out_sem.at[0])
    gate_store.start()
    arrive_far(2)
    do(UP, 4)
    up_store = pltpu.make_async_copy(acc.at[UP], up_out, out_sem.at[1])
    up_store.start()

    def x_sum(gl):
        total = part_b[x * 2 + gl].astype(jnp.float32)
        for slot in range(3):
            remote(
                part_b.at[0], rx.at[gl, slot], g_s.at[0], g_r.at[gl, slot], sibling
            ).wait_recv()
            total = total + rx[gl, slot].astype(jnp.float32)
        return total

    sy[...] = x_sum(1 - yl).astype(jnp.bfloat16)
    y_part = remote(sy, ry, h_s, h_r, partner)
    y_part.start()
    total = x_sum(yl)
    y_part.wait_recv()
    fin[...] = (total + ry[...].astype(jnp.float32)).astype(jnp.bfloat16)
    fin_store = pltpu.make_async_copy(fin, igrad_out, out_sem.at[2])
    fin_store.start()

    for cp in started:
        cp.wait_send()
    for off in OFFS:
        cond, copy = scatter(off)
        pl.when(cond)(lambda: copy().wait_send())
    y_part.wait_send()
    for cp in (gate_store, up_store, fin_store):
        cp.wait()


def per_device(*args):
    bf16, f32 = jnp.bfloat16, jnp.float32
    dma = pltpu.SemaphoreType.DMA
    hbm = pl.BlockSpec(memory_space=pl.ANY)
    return tuple(
        pl.pallas_call(
            kernel,
            out_shape=(
                jax.ShapeDtypeStruct((GROUP, FEAT), bf16),
                jax.ShapeDtypeStruct((FEAT, HID), f32),
                jax.ShapeDtypeStruct((FEAT, HID), f32),
            ),
            in_specs=[hbm] * 6,
            out_specs=(hbm,) * 3,
            scratch_shapes=[
                pltpu.VMEM((2, NZ, GROUP, HID), bf16),
                pltpu.VMEM((NZ, GROUP, FEAT), bf16),
                pltpu.VMEM((NZ, FEAT, GROUP), bf16),
                pltpu.VMEM((2, FEAT, HID), bf16),
                pltpu.VMEM((2, HID, FEAT), bf16),
                pltpu.VMEM((2, FEAT, HID), f32),
                pltpu.VMEM((NZ, GROUP, FEAT), f32),
                pltpu.VMEM((NZ, GROUP, FEAT), bf16),
                pltpu.VMEM((2, 3, GROUP, FEAT), bf16),
                pltpu.VMEM((GROUP, FEAT), bf16),
                pltpu.VMEM((GROUP, FEAT), bf16),
                pltpu.VMEM((GROUP, FEAT), bf16),
                pltpu.VMEM((3, ROWS, HID), bf16),
                dma((6,)),
                dma((2, 3, 3)), dma((2, 3, 3)),
                dma((3,)), dma((3,)),
                dma((NZ + 1,)), dma((NZ + 1,)),
                dma((2, 2, NZ)), dma((2, 2, NZ)),
                dma((7,)), dma((7,)),
                dma((NZ,)), dma((2, 3)),
                dma, dma,
                dma((3,)),
            ],
            compiler_params=pltpu.CompilerParams(
                collective_id=0, has_side_effects=True, vmem_limit_bytes=48 * 2**20
            ),
            cost_estimate=pl.CostEstimate(flops=7516192768, bytes_accessed=8 * 2**20, transcendentals=0),
            name="swiglu_bwd",
        )(*args)
    )


def solution(mesh):
    in_specs = (
        P("tensor", "dp"),
        P("dp", "tensor"),
        P("dp", "tensor"),
        P("dp", "tensor"),
        P("dp", "tensor"),
        P("dp", "tensor"),
    )
    out_specs = (P("tensor", "dp"), P("dp", "tensor"), P("dp", "tensor"))
    return jax.shard_map(
        per_device, mesh=mesh, in_specs=in_specs, out_specs=out_specs, check_vma=False
    )
```

time: 301 us -> 90.7 us (0.30)
  waiting for transfers between devices: 254 us -> 0 us
  Pallas kernels: 0 us -> 79.6 us
  matrix products: 24.1 us -> 0 us
  between operations: 13.8 us -> 0.66 us
  local copies, waits for them, and re-layouts: 3.39 us -> 10.1 us
    all_gather x3 -> x0, waiting for transfers between devices: 223 us -> none  [the longest x1 98.5 us: per_device(): lax.all_gather(gate_grad, 'dp', axis=0, tiled=True)]
    pallas_call x0 -> x1, Pallas kernels: none -> 79.6 us  [per_device(): pl.pallas_call(kernel, out_shape=(jax.ShapeDtypeStruct((GROUP, FEAT), bf1...]
    reduce_scatter x1 -> x0, waiting for transfers between devices: 29.5 us -> none  [per_device(): lax.psum_scatter(partial_terms.astype(jnp.bfloat16), 'tensor', scatter_di...]
    dot_general x4 -> x0, matrix products: 24.1 us -> none  [the longest x2 13.3 us: feature_product(): lax.dot_general(grad_rows, weight_tile, (((1,), (1,)), ((), ())), preferr...]
    unnamed x6 -> x17, local copies, waits for them, and re-layouts: 3.39 us -> 10.1 us
  transfers between devices with their start and end apart: 4 -> 0, of which waited for: 4 -> 0; matrix products, arithmetic and copies ran while one was open for 9% -> 0% of each run, Pallas kernels for 0% -> 0%
where the time goes in v1:
time: 90.7 us; the launch traced here: 90.4 us
  Pallas kernels  79.6 us (88%)
  local copies, waits for them, and re-layouts  10.1 us (11%)
    pallas_call x1, Pallas kernels, per_device(): pl.pallas_call(kernel, out_shape=(jax.ShapeDtypeStruct((GROUP, FEAT), bf1...  79.6 us
    unnamed x17, local copies, waits for them, and re-layouts  10.1 us

profile of v1, /device:TPU:20, one launch (start us, length us, event | category | flops | bytes accessed | tf_op | source)
XLA Modules:
  0.0 90.4 jit_solution(462469609953069558)
XLA Ops:
  0.6 0.0 copy-start
  0.6 1.2 %copy-done = bf16[256,1792]{1,0:T(8,128)(2,1)S(1)} copy-done((bf16[256,1792]{1,0:T(8,128)(2,1)S(1)}, bf16[256,1792]{1,0:T(8,128)(2,1)}, u32[]{:S(2)}) %copy-start) | copy-done | bytes 917528
  1.8 0.0 copy-start.1
  1.8 1.2 %copy-done.1 = bf16[256,1792]{1,0:T(8,128)(2,1)S(1)} copy-done((bf16[256,1792]{1,0:T(8,128)(2,1)S(1)}, bf16[256,1792]{1,0:T(8,128)(2,1)}, u32[]{:S(2)}) %copy-start.1) | copy-done | bytes 917528
  3.0 0.0 copy-start.2
  3.0 0.9 %copy-done.2 = bf16[64,1792]{1,0:T(8,128)(2,1)S(1)} copy-done((bf16[64,1792]{1,0:T(8,128)(2,1)S(1)}, bf16[64,1792]{1,0:T(8,128)(2,1)}, u32[]{:S(2)}) %copy-start.2) | copy-done | bytes 229400
  3.9 0.0 copy-start.3
  3.9 0.9 %copy-done.3 = bf16[64,1792]{1,0:T(8,128)(2,1)S(1)} copy-done((bf16[64,1792]{1,0:T(8,128)(2,1)S(1)}, bf16[64,1792]{1,0:T(8,128)(2,1)}, u32[]{:S(2)}) %copy-start.3) | copy-done | bytes 229400
  4.9 0.0 copy-start.4
  4.9 0.9 %copy-done.4 = bf16[64,1792]{1,0:T(8,128)(2,1)S(1)} copy-done((bf16[64,1792]{1,0:T(8,128)(2,1)S(1)}, bf16[64,1792]{1,0:T(8,128)(2,1)}, u32[]{:S(2)}) %copy-start.4) | copy-done | bytes 229400
  5.8 0.0 copy-start.5
  5.8 0.9 copy-done.5
  6.7 79.6 %swiglu_bwd.1 = (bf16[256,256]{1,0:T(8,128)(2,1)S(1)}, f32[256,1792]{1,0:T(8,128)S(1)}, f32[256,1792]{1,0:T(8,128)}) custom-call(bf16[256,256]{1,0:T(8,128)(2,1)S(1)} %copy-done.5, bf16[64,1792]{1,0:T(8,128)(2,1)S(1)} %copy-done.2, bf16[64,1792]{1,0:T(8,128)(2,1)S(1)} %copy-done.3, bf16[64,1792]{1,0:T(8,128)(2,1)S(1)} %copy-done.4, ...), custom_call_target="tpu_custom_call" | custom-call | flops 7516192768 | bytes 8388608 | tf_op jit(solution)/shard_map/swiglu_bwd/pallas_call | solution.py:317
  86.4 0.7 copy.12
  87.0 0.0 copy-start.6
  87.0 1.2 %copy.13 = f32[256,1792]{1,0:T(8,128)} copy(f32[256,1792]{1,0:T(8,128)S(1)} %get-tuple-element.7) | data formatting | bytes 3670016
  88.3 0.9 %copy-done.6 = f32[256,1792]{1,0:T(8,128)S(1)} copy-done((f32[256,1792]{1,0:T(8,128)S(1)}, f32[256,1792]{1,0:T(8,128)}, u32[]{:S(2)}) %copy-start.6) | copy-done | bytes 1835032
  89.2 1.2 %copy.14 = f32[256,1792]{1,0:T(8,128)} copy(f32[256,1792]{1,0:T(8,128)S(1)} %copy-done.6) | data formatting | bytes 3670016
Async XLA Ops:
  0.6 1.2 %copy-start = (bf16[256,1792]{1,0:T(8,128)(2,1)S(1)}, bf16[256,1792]{1,0:T(8,128)(2,1)}, u32[]{:S(2)}) copy-start(bf16[256,1792]{1,0:T(8,128)(2,1)} %gate_weight.1) | copy-start | bytes 2752516
  1.8 1.2 %copy-start.1 = (bf16[256,1792]{1,0:T(8,128)(2,1)S(1)}, bf16[256,1792]{1,0:T(8,128)(2,1)}, u32[]{:S(2)}) copy-start(bf16[256,1792]{1,0:T(8,128)(2,1)} %up_weight.1) | copy-start | bytes 2752516
  3.0 0.9 %copy-start.2 = (bf16[64,1792]{1,0:T(8,128)(2,1)S(1)}, bf16[64,1792]{1,0:T(8,128)(2,1)}, u32[]{:S(2)}) copy-start(bf16[64,1792]{1,0:T(8,128)(2,1)} %gate_pre.1) | copy-start | bytes 688132
  3.9 0.9 %copy-start.3 = (bf16[64,1792]{1,0:T(8,128)(2,1)S(1)}, bf16[64,1792]{1,0:T(8,128)(2,1)}, u32[]{:S(2)}) copy-start(bf16[64,1792]{1,0:T(8,128)(2,1)} %up_pre.1) | copy-start | bytes 688132
  4.9 0.9 %copy-start.4 = (bf16[64,1792]{1,0:T(8,128)(2,1)S(1)}, bf16[64,1792]{1,0:T(8,128)(2,1)}, u32[]{:S(2)}) copy-start(bf16[64,1792]{1,0:T(8,128)(2,1)} %hidden_grad.1) | copy-start | bytes 688132
  5.8 0.9 %copy-start.5 = (bf16[256,256]{1,0:T(8,128)(2,1)S(1)}, bf16[256,256]{1,0:T(8,128)(2,1)}, u32[]{:S(2)}) copy-start(bf16[256,256]{1,0:T(8,128)(2,1)} %inputs.1) | copy-start | bytes 393220
  87.0 2.2 %copy-start.6 = (f32[256,1792]{1,0:T(8,128)S(1)}, f32[256,1792]{1,0:T(8,128)}, u32[]{:S(2)}) copy-start(f32[256,1792]{1,0:T(8,128)} %get-tuple-element.8) | copy-start | bytes 5505028

commit v2 on v1

--- a/solution.py
+++ b/solution.py
@@ -16,15 +16,16 @@
 NZ = 8
 NX = 4
 GATE, UP = 0, 1
+VMEM_BYTES = 56 * 2**20
 SCALE = 1.0 / math.sqrt(2048)
 OFFS = (0, -1, 1, -2, 2, -3, 3, 4)
 
 
 def kernel(
     inputs, gate_pre, up_pre, hidden_grad, gate_weight, up_weight,
-    igrad_out, gate_out, up_out,
-    grads, xs, xt, w, wt, acc, part, part_b, rx, ry, sy, fin, pre,
-    loc, z_s, z_r, f_s, f_r, y_s, y_r, c_s, c_r, x_s, x_r, g_s, g_r, h_s, h_r, out_sem,
+    igrad_out, gate_acc, up_acc,
+    grads, xs, xt, w, wt, part, part_b, rx, ry, sy, pre,
+    loc, z_s, z_r, f_s, f_r, y_s, y_r, c_s, c_r, x_s, x_r, g_s, g_r, h_s, h_r,
 ):
     dp, tensor = lax.axis_index("dp"), lax.axis_index("tensor")
     z, yh, c = dp // 4, (dp // 2) % 2, dp % 2
@@ -151,46 +152,47 @@
         y_copy(GATE, off).wait_recv()
         go(c_copy(GATE, 1, off))
 
-    def from_sibling(kind, off):
-        for far in (0, 1):
-            c_copy(kind, far, off).wait_recv()
+    def from_sibling(kind, far, off):
+        c_copy(kind, far, off).wait_recv()
 
     def wgrad(kind, off):
         g = group(off)
+        acc = (gate_acc, up_acc)[kind]
         for half in (0, 1):
             cols = pl.ds(half * 896, 896)
             prod = jnp.dot(xt[g], grads[kind, g, :, cols], preferred_element_type=jnp.float32)
             if off != 0:
-                prod = acc[kind, :, cols] + prod
+                prod = acc[:, cols] + prod
             if off == 4:
                 prod = prod * SCALE
-            acc[kind, :, cols] = prod
+            acc[:, cols] = prod
 
     def igrad(kind, off):
         g = group(off)
-        prod = jnp.dot(grads[kind, g], wt[kind], preferred_element_type=jnp.float32)
-        if kind == GATE:
-            part[g] = prod
-        else:
-            part_b[g] = (part[g] + prod).astype(jnp.bfloat16)
-
-    def scatter(off):
+        part[g] = jnp.dot(grads[kind, g], wt[kind], preferred_element_type=jnp.float32)
+
+    def finish(off, far):
+        g = group(off)
+        rows = pl.ds(pl.multiple_of((1 - yh if far else yh) * 128, 128), 128)
+        prod = jnp.dot(grads[UP, g, rows, :], wt[UP], preferred_element_type=jnp.float32)
+        part_b[g, rows, :] = (part[g, rows, :] + prod).astype(jnp.bfloat16)
+        cond, copy = scatter(off, far)
+        pl.when(cond)(lambda: copy().start())
+
+    def scatter(off, far):
         g = group(off)
         gx, gl = g // 2, g % 2
         i = off % NZ
         slot = (x - gx + NX) % NX - 1
+        rows = pl.ds(pl.multiple_of((1 - yh if far else yh) * 128, 128), 128)
 
         def copy():
             return remote(
-                part_b.at[g], rx.at[gl, slot], g_s.at[i], g_r.at[gl, slot],
+                part_b.at[g, rows, :], rx.at[gl, slot, rows, :], g_s.at[i, far], g_r.at[gl, slot, far],
                 {"dp": dp, "tensor": gx * 2 + yl},
             )
 
         return x != gx, copy
-
-    def send_part(off):
-        cond, copy = scatter(off)
-        pl.when(cond)(lambda: copy().start())
 
     for way in (0, 1):
         go(z_copy(way, 0, 0))
@@ -213,9 +215,6 @@
             wt[kind, cols, :] = w[kind, :, cols].T
         return 0
 
-    x_copy(0).wait_recv()
-    for slot in (4, 5, 6):
-        go(x_copy(slot))
     lax.fori_loop(0, HID // 256, flip_w, 0)
 
     arrive_z(0, 0)
@@ -223,8 +222,10 @@
     for way in (0, 1):
         go(z_copy(way, 2, 0))
     go(c_copy(UP, 1, 0))
+    x_copy(0).wait_recv()
+    for slot in (4, 5, 6):
+        go(x_copy(slot))
     arrive_z(1, 0)
-    arrive_y(0)
 
     x_load.wait()
     for slot in range(1, 7):
@@ -237,75 +238,104 @@
     lax.fori_loop(0, NZ, flip_x, 0)
 
     def do(kind, off):
-        from_sibling(kind, off)
-        igrad(kind, off)
-        if kind == UP:
-            send_part(off)
+        if kind == GATE:
+            from_sibling(GATE, 0, off)
+            from_sibling(GATE, 1, off)
+            igrad(GATE, off)
+        else:
+            for far in (0, 1):
+                from_sibling(UP, far, off)
+                finish(off, far)
         wgrad(kind, off)
 
+    arrive_y(0)
+    arrive_z(0, 1)
     do(GATE, 0)
     do(UP, 0)
-    arrive_z(0, 1)
     arrive_y(-1)
     arrive_z(2, 0)
+    do(GATE, -1)
     arrive_y(1)
-    do(GATE, -1)
+    arrive_z(1, 1)
+    do(UP, -1)
     do(GATE, 1)
-    arrive_z(1, 1)
+    do(UP, 1)
     arrive_y(-2)
-    do(UP, -1)
-    do(UP, 1)
     arrive_z(0, 2)
+    do(GATE, -2)
     arrive_y(2)
-    do(GATE, -2)
+    arrive_z(2, 1)
     do(GATE, 2)
-    arrive_z(2, 1)
     arrive_y(-3)
+    arrive_z(1, 2)
     do(UP, -2)
+    arrive_far(0)
     do(UP, 2)
-    arrive_z(1, 2)
     arrive_y(3)
     do(GATE, -3)
     do(GATE, 3)
-    arrive_far(0)
     arrive_z(2, 2)
     do(UP, -3)
+    arrive_y(4)
     do(UP, 3)
     arrive_far(1)
-    arrive_y(4)
     do(GATE, 4)
-    gate_store = pltpu.make_async_copy(acc.at[GATE], gate_out, out_sem.at[0])
-    gate_store.start()
+    from_sibling(UP, 0, 4)
+    finish(4, 0)
     arrive_far(2)
-    do(UP, 4)
-    up_store = pltpu.make_async_copy(acc.at[UP], up_out, out_sem.at[1])
-    up_store.start()
-
-    def x_sum(gl):
-        total = part_b[x * 2 + gl].astype(jnp.float32)
+    from_sibling(UP, 1, 4)
+    finish(4, 1)
+    wgrad(UP, 4)
+
+    def half(far):
+        return pl.ds(pl.multiple_of((1 - yh if far else yh) * 128, 128), 128)
+
+    def x_sum(gl, far):
+        rows = half(far)
+        total = part_b[x * 2 + gl, rows, :].astype(jnp.float32)
         for slot in range(3):
-            remote(
-                part_b.at[0], rx.at[gl, slot], g_s.at[0], g_r.at[gl, slot], sibling
-            ).wait_recv()
-            total = total + rx[gl, slot].astype(jnp.float32)
+            b = rx.at[gl, slot, rows, :]
+            remote(b, b, g_s.at[0, 0], g_r.at[gl, slot, far], sibling).wait_recv()
+            total = total + rx[gl, slot, rows, :].astype(jnp.float32)
         return total
 
-    sy[...] = x_sum(1 - yl).astype(jnp.bfloat16)
-    y_part = remote(sy, ry, h_s, h_r, partner)
-    y_part.start()
-    total = x_sum(yl)
-    y_part.wait_recv()
-    fin[...] = (total + ry[...].astype(jnp.float32)).astype(jnp.bfloat16)
-    fin_store = pltpu.make_async_copy(fin, igrad_out, out_sem.at[2])
-    fin_store.start()
+    def y_part(far):
+        rows = half(far)
+        return remote(sy.at[rows, :], ry.at[rows, :], h_s.at[far], h_r.at[far], partner)
+
+    def sum_half(far):
+        rows = half(far)
+        sy[rows, :] = x_sum(1 - yl, far).astype(jnp.bfloat16)
+        y_part(far).start()
+        part[0, rows, :] = x_sum(yl, far)
+
+    def end_half(far):
+        rows = half(far)
+        y_part(far).wait_recv()
+        igrad_out[rows, :] = (part[0, rows, :] + ry[rows, :].astype(jnp.float32)).astype(jnp.bfloat16)
+
+    sum_half(0)
+    sum_half(1)
+    end_half(0)
+    end_half(1)
 
     for cp in started:
         cp.wait_send()
     for off in OFFS:
-        cond, copy = scatter(off)
-        pl.when(cond)(lambda: copy().wait_send())
-    y_part.wait_send()
-    for cp in (gate_store, up_store, fin_store):
+        for far in (0, 1):
+            cond, copy = scatter(off, far)
+            pl.when(cond)(lambda: copy().wait_send())
+    for far in (0, 1):
+        y_part(far).wait_send()
+
+
+def write_out(*refs):
+    n = len(refs) // 2
+    sem = refs[-1]
+    copies = [pltpu.make_async_copy(refs[i], refs[n + i], sem.at[i]) for i in range(n)]
+    for cp in copies:
+        cp.start()
+    for cp in copies:
         cp.wait()
 
 
@@ -313,46 +343,50 @@
     bf16, f32 = jnp.bfloat16, jnp.float32
     dma = pltpu.SemaphoreType.DMA
     hbm = pl.BlockSpec(memory_space=pl.ANY)
+    vmem = pl.BlockSpec(memory_space=pltpu.VMEM)
+    outs = (((GROUP, FEAT), bf16), ((FEAT, HID), f32), ((FEAT, HID), f32))
+    held = pl.pallas_call(
+        kernel,
+        out_shape=tuple(pltpu.VMEM(*o) for o in outs),
+        in_specs=[hbm] * 6,
+        out_specs=(vmem,) * 3,
+        scratch_shapes=[
+            pltpu.VMEM((2, NZ, GROUP, HID), bf16),
+            pltpu.VMEM((NZ, GROUP, FEAT), bf16),
+            pltpu.VMEM((NZ, FEAT, GROUP), bf16),
+            pltpu.VMEM((2, FEAT, HID), bf16),
+            pltpu.VMEM((2, HID, FEAT), bf16),
+            pltpu.VMEM((NZ, GROUP, FEAT), f32),
+            pltpu.VMEM((NZ, GROUP, FEAT), bf16),
+            pltpu.VMEM((2, 3, GROUP, FEAT), bf16),
+            pltpu.VMEM((GROUP, FEAT), bf16),
+            pltpu.VMEM((GROUP, FEAT), bf16),
+            pltpu.VMEM((3, ROWS, HID), bf16),
+            dma((6,)),
+            dma((2, 3, 3)), dma((2, 3, 3)),
+            dma((3,)), dma((3,)),
+            dma((NZ + 1,)), dma((NZ + 1,)),
+            dma((2, 2, NZ)), dma((2, 2, NZ)),
+            dma((7,)), dma((7,)),
+            dma((NZ, 2)), dma((2, 3, 2)),
+            dma((2,)), dma((2,)),
+        ],
+        compiler_params=pltpu.CompilerParams(
+            collective_id=0, has_side_effects=True, vmem_limit_bytes=VMEM_BYTES
+        ),
+        cost_estimate=pl.CostEstimate(flops=7516192768, bytes_accessed=8 * 2**20, transcendentals=0),
+        name="swiglu_bwd",
+    )(*args)
     return tuple(
         pl.pallas_call(
-            kernel,
-            out_shape=(
-                jax.ShapeDtypeStruct((GROUP, FEAT), bf16),
-                jax.ShapeDtypeStruct((FEAT, HID), f32),
-                jax.ShapeDtypeStruct((FEAT, HID), f32),
-            ),
-            in_specs=[hbm] * 6,
+            write_out,
+            out_shape=tuple(jax.ShapeDtypeStruct(*o) for o in outs),
+            in_specs=[hbm] * 3,
             out_specs=(hbm,) * 3,
-            scratch_shapes=[
-                pltpu.VMEM((2, NZ, GROUP, HID), bf16),
-                pltpu.VMEM((NZ, GROUP, FEAT), bf16),
-                pltpu.VMEM((NZ, FEAT, GROUP), bf16),
-                pltpu.VMEM((2, FEAT, HID), bf16),
-                pltpu.VMEM((2, HID, FEAT), bf16),
-                pltpu.VMEM((2, FEAT, HID), f32),
-                pltpu.VMEM((NZ, GROUP, FEAT), f32),
-                pltpu.VMEM((NZ, GROUP, FEAT), bf16),
-                pltpu.VMEM((2, 3, GROUP, FEAT), bf16),
-                pltpu.VMEM((GROUP, FEAT), bf16),
-                pltpu.VMEM((GROUP, FEAT), bf16),
-                pltpu.VMEM((GROUP, FEAT), bf16),
-                pltpu.VMEM((3, ROWS, HID), bf16),
-                dma((6,)),
-                dma((2, 3, 3)), dma((2, 3, 3)),
-                dma((3,)), dma((3,)),
-                dma((NZ + 1,)), dma((NZ + 1,)),
-                dma((2, 2, NZ)), dma((2, 2, NZ)),
-                dma((7,)), dma((7,)),
-                dma((NZ,)), dma((2, 3)),
-                dma, dma,
-                dma((3,)),
-            ],
-            compiler_params=pltpu.CompilerParams(
-                collective_id=0, has_side_effects=True, vmem_limit_bytes=48 * 2**20
-            ),
-            cost_estimate=pl.CostEstimate(flops=7516192768, bytes_accessed=8 * 2**20, transcendentals=0),
-            name="swiglu_bwd",
-        )(*args)
+            scratch_shapes=[dma((3,))],
+            compiler_params=pltpu.CompilerParams(vmem_limit_bytes=4 * 2**20),
+            name="write_out",
+        )(*held)
     )
 
 

time: 90.7 us -> 78.1 us (0.86)
  local copies, waits for them, and re-layouts: 10.1 us -> 0 us
  Pallas kernels: 79.6 us -> 76.9 us
    unnamed x17 -> x0, local copies, waits for them, and re-layouts: 10.1 us -> none
    pallas_call x1 -> x2, Pallas kernels: 79.6 us -> 76.9 us  [the longest x1 75 us: per_device(): pl.pallas_call(kernel, out_shape=tuple((pltpu.VMEM(*o) for o in outs)), i...]
where the time goes in v2:
time: 78.1 us; the launch traced here: 77.5 us
  Pallas kernels  76.9 us (98%)
    pallas_call x1, Pallas kernels, per_device(): pl.pallas_call(kernel, out_shape=tuple((pltpu.VMEM(*o) for o in outs)), i...  75 us
    pallas_call x1, Pallas kernels, per_device(): pl.pallas_call(write_out, out_shape=tuple((jax.ShapeDtypeStruct(*o) for o...  1.9 us

profile of v2, /device:TPU:20, one launch (start us, length us, event | category | flops | bytes accessed | tf_op | source)
XLA Modules:
  0.0 77.5 jit_solution(6904629320650064092)
XLA Ops:
  0.6 75.0 %swiglu_bwd.1 = (bf16[256,256]{1,0:T(8,128)(2,1)S(1)}, f32[256,1792]{1,0:T(8,128)S(1)}, f32[256,1792]{1,0:T(8,128)S(1)}) custom-call(bf16[256,256]{1,0:T(8,128)(2,1)} %inputs.1, bf16[64,1792]{1,0:T(8,128)(2,1)} %gate_pre.1, bf16[64,1792]{1,0:T(8,128)(2,1)} %up_pre.1, bf16[64,1792]{1,0:T(8,128)(2,1)} %hidden_grad.1, bf16[256,1792]{1,0:T(8,128)(2,1)} %gate_weight.1, ...), custom_call_target="tpu_custom_call" | custom-call | flops 7516192768 | bytes 8388608 | tf_op jit(solution)/shard_map/swiglu_bwd/pallas_call | solution.py:348
  75.6 1.9 %write_out.1 = (bf16[256,256]{1,0:T(8,128)(2,1)}, f32[256,1792]{1,0:T(8,128)}, f32[256,1792]{1,0:T(8,128)}) custom-call(bf16[256,256]{1,0:T(8,128)(2,1)S(1)} %get-tuple-element.6.refs_0_, f32[256,1792]{1,0:T(8,128)S(1)} %get-tuple-element.7.refs_1_, f32[256,1792]{1,0:T(8,128)S(1)} %get-tuple-element.8.refs_2_), custom_call_target="tpu_custom_call" | custom-call | tf_op jit(solution)/shard_map/write_out/pallas_call | solution.py:381

commit v3 on v2

--- a/solution.py
+++ b/solution.py
@@ -15,6 +15,8 @@
 FEAT = 256
 NZ = 8
 NX = 4
+PIECE = 128 // NX
+PARTS = 1
 GATE, UP = 0, 1
 VMEM_BYTES = 56 * 2**20
 SCALE = 1.0 / math.sqrt(2048)
@@ -24,7 +26,7 @@
 def kernel(
     inputs, gate_pre, up_pre, hidden_grad, gate_weight, up_weight,
     igrad_out, gate_acc, up_acc,
-    grads, xs, xt, w, wt, part, part_b, rx, ry, sy, pre,
+    grads, xs, xt, w, wt, part, part_b, rx, sums, fin, pre,
     loc, z_s, z_r, f_s, f_r, y_s, y_r, c_s, c_r, x_s, x_r, g_s, g_r, h_s, h_r,
 ):
     dp, tensor = lax.axis_index("dp"), lax.axis_index("tensor")
@@ -100,7 +102,8 @@
         cp.start()
 
     barrier = pltpu.get_barrier_semaphore()
-    peers = [at_z(1), at_z(-1), opposite, sibling, partner, at_x(1), at_x(2), at_x(3)]
+    peers = [at_z(1), at_z(-1), opposite, sibling]
+    peers += [{"dp": dp, "tensor": (tensor + i) % NZ} for i in range(1, NZ)]
     for peer in peers:
         pl.semaphore_signal(barrier, inc=1, device_id=peer, device_id_type=MESH)
 
@@ -128,14 +131,19 @@
         cp.start()
         started.append(cp)
 
+    def forward(stream, hop):
+        if hop < 2:
+            for way in (0, 1):
+                go(z_copy(way, stream, hop + 1))
+        else:
+            go(far_copy(stream))
+
     def arrive_z(stream, hop):
         kind, far = STREAM[stream]
         for way in (0, 1):
             z_copy(way, stream, hop).wait_recv()
-            if hop < 2:
-                go(z_copy(way, stream, hop + 1))
-        if hop == 2:
-            go(far_copy(stream))
+        if kind == GATE:
+            forward(stream, hop)
         for off in (-(hop + 1), hop + 1):
             if kind == GATE:
                 go(y_copy(GATE, off))
@@ -167,32 +175,76 @@
                 prod = prod * SCALE
             acc[:, cols] = prod
 
-    def igrad(kind, off):
+    def igrad(off):
         g = group(off)
-        part[g] = jnp.dot(grads[kind, g], wt[kind], preferred_element_type=jnp.float32)
-
-    def finish(off, far):
+        part[g] = jnp.dot(grads[GATE, g], wt[GATE], preferred_element_type=jnp.float32)
+
+    def piece(step):
+        return pl.ds(pl.multiple_of(((x + step) % NX) * PIECE, PIECE), PIECE)
+
+    def g_copy(off, step):
+        i = off % NZ
+        return remote(
+            part_b.at[group(off), :, piece(step), :], rx.at[i, step - 1],
+            g_s.at[i, step - 1], g_r.at[i, step - 1], at_x(step),
+        )
+
+    def finish(off):
         g = group(off)
-        rows = pl.ds(pl.multiple_of((1 - yh if far else yh) * 128, 128), 128)
+        prod = jnp.dot(grads[UP, g], wt[UP], preferred_element_type=jnp.float32)
+        prod = (part[g] + prod).astype(jnp.bfloat16)
+        for h in (0, 1):
+            part_b[g, h] = prod[h * 128 : (h + 1) * 128]
+        for step in (1, 2, 3):
+            go(g_copy(off, step))
+
+    def h_copy(off, h):
+        return remote(
+            sums.at[off % NZ, h], fin.at[tensor, h], h_s.at[off % NZ, h], h_r.at[tensor, h],
+            {"dp": dp, "tensor": group(off)},
+        )
+
+    def to_owner(off, h, total):
+        sums[off % NZ, h] = total.astype(jnp.bfloat16)
+        pl.when(tensor != group(off))(lambda: h_copy(off, h).start())
+
+        @pl.when(tensor == group(off))
+        def _():
+            fin[tensor, h] = total.astype(jnp.bfloat16)
+
+    def collect(off):
+        total = part_b[group(off), :, piece(0), :].astype(jnp.float32)
+        for step in (1, 2, 3):
+            g_copy(off, step).wait_recv()
+            total = total + rx[off % NZ, step - 1].astype(jnp.float32)
+        for h in (0, 1):
+            to_owner(off, h, total[h])
+
+    def last_half(far):
+        return 1 - yh if far else yh
+
+    def last_copy(far, step):
+        h = last_half(far)
+        return remote(
+            part_b.at[group(4), h, piece(step), :], rx.at[4, step - 1, h],
+            g_s.at[4 + 4 * far, step - 1], g_r.at[4 + 4 * far, step - 1], at_x(step),
+        )
+
+    def last_finish(far):
+        g, h = group(4), last_half(far)
+        rows = pl.ds(pl.multiple_of(h * 128, 128), 128)
         prod = jnp.dot(grads[UP, g, rows, :], wt[UP], preferred_element_type=jnp.float32)
-        part_b[g, rows, :] = (part[g, rows, :] + prod).astype(jnp.bfloat16)
-        cond, copy = scatter(off, far)
-        pl.when(cond)(lambda: copy().start())
-
-    def scatter(off, far):
-        g = group(off)
-        gx, gl = g // 2, g % 2
-        i = off % NZ
-        slot = (x - gx + NX) % NX - 1
-        rows = pl.ds(pl.multiple_of((1 - yh if far else yh) * 128, 128), 128)
-
-        def copy():
-            return remote(
-                part_b.at[g, rows, :], rx.at[gl, slot, rows, :], g_s.at[i, far], g_r.at[gl, slot, far],
-                {"dp": dp, "tensor": gx * 2 + yl},
-            )
-
-        return x != gx, copy
+        part_b[g, h] = (part[g, rows, :] + prod).astype(jnp.bfloat16)
+        for step in (1, 2, 3):
+            go(last_copy(far, step))
+
+    def collect_last(far):
+        h = last_half(far)
+        total = part_b[group(4), h, piece(0), :].astype(jnp.float32)
+        for step in (1, 2, 3):
+            last_copy(far, step).wait_recv()
+            total = total + rx[4, step - 1, h].astype(jnp.float32)
+        to_owner(4, h, total)
 
     for way in (0, 1):
         go(z_copy(way, 0, 0))
@@ -237,102 +289,110 @@
 
     lax.fori_loop(0, NZ, flip_x, 0)
 
+    def from_both(kind, off):
+        for far in (0, 1):
+            from_sibling(kind, far, off)
+
     def do(kind, off):
+        from_both(kind, off)
         if kind == GATE:
-            from_sibling(GATE, 0, off)
-            from_sibling(GATE, 1, off)
-            igrad(GATE, off)
+            igrad(off)
         else:
-            for far in (0, 1):
-                from_sibling(UP, far, off)
-                finish(off, far)
+            finish(off)
         wgrad(kind, off)
 
     arrive_y(0)
     arrive_z(0, 1)
+    forward(1, 0)
     do(GATE, 0)
     do(UP, 0)
     arrive_y(-1)
     arrive_z(2, 0)
     do(GATE, -1)
+    do(UP, -1)
     arrive_y(1)
-    arrive_z(1, 1)
-    do(UP, -1)
+    arrive_z(0, 2)
+    forward(2, 0)
     do(GATE, 1)
     do(UP, 1)
     arrive_y(-2)
-    arrive_z(0, 2)
+    arrive_z(1, 1)
+    forward(1, 1)
+    collect(0)
     do(GATE, -2)
+    arrive_far(0)
     arrive_y(2)
+    collect(-1)
+    collect(1)
+    do(GATE, 2)
     arrive_z(2, 1)
-    do(GATE, 2)
+    forward(2, 1)
     arrive_y(-3)
+    do(UP, -2)
+    do(GATE, -3)
     arrive_z(1, 2)
-    do(UP, -2)
-    arrive_far(0)
+    forward(1, 2)
     do(UP, 2)
     arrive_y(3)
-    do(GATE, -3)
     do(GATE, 3)
     arrive_z(2, 2)
-    do(UP, -3)
+    forward(2, 2)
     arrive_y(4)
-    do(UP, 3)
+    collect(-2)
+    collect(2)
+    from_both(UP, -3)
+    finish(-3)
+    from_both(UP, 3)
+    finish(3)
     arrive_far(1)
-    do(GATE, 4)
+    from_both(GATE, 4)
+    igrad(4)
+    wgrad(UP, -3)
     from_sibling(UP, 0, 4)
-    finish(4, 0)
+    last_finish(0)
     arrive_far(2)
+    wgrad(UP, 3)
     from_sibling(UP, 1, 4)
-    finish(4, 1)
+    last_finish(1)
+    collect(-3)
+    collect(3)
+    wgrad(GATE, 4)
+    collect_last(0)
+    collect_last(1)
     wgrad(UP, 4)
 
-    def half(far):
-        return pl.ds(pl.multiple_of((1 - yh if far else yh) * 128, 128), 128)
-
-    def x_sum(gl, far):
-        rows = half(far)
-        total = part_b[x * 2 + gl, rows, :].astype(jnp.float32)
-        for slot in range(3):
-            b = rx.at[gl, slot, rows, :]
-            remote(b, b, g_s.at[0, 0], g_r.at[gl, slot, far], sibling).wait_recv()
-            total = total + rx[gl, slot, rows, :].astype(jnp.float32)
-        return total
-
-    def y_part(far):
-        rows = half(far)
-        return remote(sy.at[rows, :], ry.at[rows, :], h_s.at[far], h_r.at[far], partner)
-
-    def sum_half(far):
-        rows = half(far)
-        sy[rows, :] = x_sum(1 - yl, far).astype(jnp.bfloat16)
-        y_part(far).start()
-        part[0, rows, :] = x_sum(yl, far)
-
-    def end_half(far):
-        rows = half(far)
-        y_part(far).wait_recv()
-        igrad_out[rows, :] = (part[0, rows, :] + ry[rows, :].astype(jnp.float32)).astype(jnp.bfloat16)
-
-    sum_half(0)
-    sum_half(1)
-    end_half(0)
-    end_half(1)
+    def arrived(i, _):
+        @pl.when(i != tensor)
+        def _():
+            for h in (0, 1):
+                remote(fin.at[i, h], fin.at[i, h], h_s.at[0, h], h_r.at[i, h], sibling).wait_recv()
+
+        return 0
+
+    lax.fori_loop(0, NZ, arrived, 0)
+    for i in range(NX):
+        total = fin[2 * i].astype(jnp.float32) + fin[2 * i + 1].astype(jnp.float32)
+        for h in (0, 1):
+            igrad_out[h * 128 + i * PIECE : h * 128 + (i + 1) * PIECE, :] = total[h].astype(jnp.bfloat16)
 
     for cp in started:
         cp.wait_send()
     for off in OFFS:
-        for far in (0, 1):
-            cond, copy = scatter(off, far)
-            pl.when(cond)(lambda: copy().wait_send())
-    for far in (0, 1):
-        y_part(far).wait_send()
+        @pl.when(tensor != group(off))
+        def _():
+            for h in (0, 1):
+                h_copy(off, h).wait_send()
 
 
 def write_out(*refs):
     n = len(refs) // 2
     sem = refs[-1]
-    copies = [pltpu.make_async_copy(refs[i], refs[n + i], sem.at[i]) for i in range(n)]
+    copies = []
+    for i in range(n):
+        rows = refs[i].shape[0] // PARTS
+        for j in range(PARTS):
+            at = pl.ds(j * rows, rows)
+            copies.append(pltpu.make_async_copy(refs[i].at[at, :], refs[n + i].at[at, :], sem.at[i, j]))
     for cp in copies:
         cp.start()
     for cp in copies:
@@ -357,10 +417,10 @@
             pltpu.VMEM((2, FEAT, HID), bf16),
             pltpu.VMEM((2, HID, FEAT), bf16),
             pltpu.VMEM((NZ, GROUP, FEAT), f32),
-            pltpu.VMEM((NZ, GROUP, FEAT), bf16),
-            pltpu.VMEM((2, 3, GROUP, FEAT), bf16),
-            pltpu.VMEM((GROUP, FEAT), bf16),
-            pltpu.VMEM((GROUP, FEAT), bf16),
+            pltpu.VMEM((NZ, 2, 128, FEAT), bf16),
+            pltpu.VMEM((NZ, 3, 2, PIECE, FEAT), bf16),
+            pltpu.VMEM((NZ, 2, PIECE, FEAT), bf16),
+            pltpu.VMEM((NZ, 2, PIECE, FEAT), bf16),
             pltpu.VMEM((3, ROWS, HID), bf16),
             dma((6,)),
             dma((2, 3, 3)), dma((2, 3, 3)),
@@ -368,8 +428,8 @@
             dma((NZ + 1,)), dma((NZ + 1,)),
             dma((2, 2, NZ)), dma((2, 2, NZ)),
             dma((7,)), dma((7,)),
-            dma((NZ, 2)), dma((2, 3, 2)),
-            dma((2,)), dma((2,)),
+            dma((NZ + 1, 3)), dma((NZ + 1, 3)),
+            dma((NZ, 2)), dma((NZ, 2)),
         ],
         compiler_params=pltpu.CompilerParams(
             collective_id=0, has_side_effects=True, vmem_limit_bytes=VMEM_BYTES
@@ -383,7 +443,7 @@
             out_shape=tuple(jax.ShapeDtypeStruct(*o) for o in outs),
             in_specs=[hbm] * 3,
             out_specs=(hbm,) * 3,
-            scratch_shapes=[dma((3,))],
+            scratch_shapes=[dma((3, PARTS))],
             compiler_params=pltpu.CompilerParams(vmem_limit_bytes=4 * 2**20),
             name="write_out",
         )(*held)

time: 78.1 us -> 75.4 us (0.965)
  Pallas kernels: 76.9 us -> 74.3 us
    pallas_call x1, Pallas kernels: 75 us -> 72.4 us  [per_device(): pl.pallas_call(kernel, out_shape=tuple((pltpu.VMEM(*o) for o in outs)), i...]
where the time goes in v3:
time: 75.4 us; the launch traced here: 75 us
  Pallas kernels  74.3 us (99%)
    pallas_call x1, Pallas kernels, per_device(): pl.pallas_call(kernel, out_shape=tuple((pltpu.VMEM(*o) for o in outs)), i...  72.4 us
    pallas_call x1, Pallas kernels, per_device(): pl.pallas_call(write_out, out_shape=tuple((jax.ShapeDtypeStruct(*o) for o...  1.9 us

profile of v3, /device:TPU:20, one launch (start us, length us, event | category | flops | bytes accessed | tf_op | source)
XLA Modules:
  0.0 75.0 jit_solution(13571695244342382804)
XLA Ops:
  0.6 72.4 %swiglu_bwd.1 = (bf16[256,256]{1,0:T(8,128)(2,1)S(1)}, f32[256,1792]{1,0:T(8,128)S(1)}, f32[256,1792]{1,0:T(8,128)S(1)}) custom-call(bf16[256,256]{1,0:T(8,128)(2,1)} %inputs.1, bf16[64,1792]{1,0:T(8,128)(2,1)} %gate_pre.1, bf16[64,1792]{1,0:T(8,128)(2,1)} %up_pre.1, bf16[64,1792]{1,0:T(8,128)(2,1)} %hidden_grad.1, bf16[256,1792]{1,0:T(8,128)(2,1)} %gate_weight.1, ...), custom_call_target="tpu_custom_call" | custom-call | flops 7516192768 | bytes 8388608 | tf_op jit(solution)/shard_map/swiglu_bwd/pallas_call | solution.py:408
  73.0 1.9 %write_out.1 = (bf16[256,256]{1,0:T(8,128)(2,1)}, f32[256,1792]{1,0:T(8,128)}, f32[256,1792]{1,0:T(8,128)}) custom-call(bf16[256,256]{1,0:T(8,128)(2,1)S(1)} %get-tuple-element.6.refs_0_, f32[256,1792]{1,0:T(8,128)S(1)} %get-tuple-element.7.refs_1_, f32[256,1792]{1,0:T(8,128)S(1)} %get-tuple-element.8.refs_2_), custom_call_target="tpu_custom_call" | custom-call | tf_op jit(solution)/shard_map/write_out/pallas_call | solution.py:441

commit v4 on v3

--- a/solution.py
+++ b/solution.py
@@ -324,9 +324,9 @@
     arrive_y(2)
     collect(-1)
     collect(1)
-    do(GATE, 2)
     arrive_z(2, 1)
     forward(2, 1)
+    do(GATE, 2)
     arrive_y(-3)
     do(UP, -2)
     do(GATE, -3)
@@ -334,30 +334,32 @@
     forward(1, 2)
     do(UP, 2)
     arrive_y(3)
-    do(GATE, 3)
     arrive_z(2, 2)
     forward(2, 2)
+    do(GATE, 3)
+    from_both(UP, -3)
+    finish(-3)
     arrive_y(4)
+    arrive_far(1)
+    from_both(UP, 3)
+    finish(3)
     collect(-2)
     collect(2)
-    from_both(UP, -3)
-    finish(-3)
-    from_both(UP, 3)
-    finish(3)
-    arrive_far(1)
     from_both(GATE, 4)
     igrad(4)
-    wgrad(UP, -3)
     from_sibling(UP, 0, 4)
     last_finish(0)
     arrive_far(2)
-    wgrad(UP, 3)
+    wgrad(UP, -3)
     from_sibling(UP, 1, 4)
     last_finish(1)
     collect(-3)
     collect(3)
+    wgrad(UP, 3)
+    collect_last(0)
     wgrad(GATE, 4)
-    collect_last(0)
+    for cp in started:
+        cp.wait_send()
     collect_last(1)
     wgrad(UP, 4)
 
@@ -375,8 +377,6 @@
         for h in (0, 1):
             igrad_out[h * 128 + i * PIECE : h * 128 + (i + 1) * PIECE, :] = total[h].astype(jnp.bfloat16)
 
-    for cp in started:
-        cp.wait_send()
     for off in OFFS:
         @pl.when(tensor != group(off))
         def _():

time: 75.4 us -> 74.8 us (level)
  no operation moved by 1% of the time
where the time goes in v4:
time: 74.8 us; the launch traced here: 74.7 us
  Pallas kernels  74 us (99%)
    pallas_call x1, Pallas kernels, per_device(): pl.pallas_call(kernel, out_shape=tuple((pltpu.VMEM(*o) for o in outs)), i...  72.1 us
    pallas_call x1, Pallas kernels, per_device(): pl.pallas_call(write_out, out_shape=tuple((jax.ShapeDtypeStruct(*o) for o...  1.9 us

profile of v4, /device:TPU:20, one launch (start us, length us, event | category | flops | bytes accessed | tf_op | source)
XLA Modules:
  0.0 74.7 jit_solution(6920915339691466815)
XLA Ops:
  0.6 72.1 %swiglu_bwd.1 = (bf16[256,256]{1,0:T(8,128)(2,1)S(1)}, f32[256,1792]{1,0:T(8,128)S(1)}, f32[256,1792]{1,0:T(8,128)S(1)}) custom-call(bf16[256,256]{1,0:T(8,128)(2,1)} %inputs.1, bf16[64,1792]{1,0:T(8,128)(2,1)} %gate_pre.1, bf16[64,1792]{1,0:T(8,128)(2,1)} %up_pre.1, bf16[64,1792]{1,0:T(8,128)(2,1)} %hidden_grad.1, bf16[256,1792]{1,0:T(8,128)(2,1)} %gate_weight.1, ...), custom_call_target="tpu_custom_call" | custom-call | flops 7516192768 | bytes 8388608 | tf_op jit(solution)/shard_map/swiglu_bwd/pallas_call | solution.py:408
  72.8 1.9 %write_out.1 = (bf16[256,256]{1,0:T(8,128)(2,1)}, f32[256,1792]{1,0:T(8,128)}, f32[256,1792]{1,0:T(8,128)}) custom-call(bf16[256,256]{1,0:T(8,128)(2,1)S(1)} %get-tuple-element.6.refs_0_, f32[256,1792]{1,0:T(8,128)S(1)} %get-tuple-element.7.refs_1_, f32[256,1792]{1,0:T(8,128)S(1)} %get-tuple-element.8.refs_2_), custom_call_target="tpu_custom_call" | custom-call | tf_op jit(solution)/shard_map/write_out/pallas_call | solution.py:441

commit v5 on v4

--- a/solution.py
+++ b/solution.py
@@ -357,11 +357,11 @@
     collect(3)
     wgrad(UP, 3)
     collect_last(0)
+    collect_last(1)
     wgrad(GATE, 4)
+    wgrad(UP, 4)
     for cp in started:
         cp.wait_send()
-    collect_last(1)
-    wgrad(UP, 4)
 
     def arrived(i, _):
         @pl.when(i != tensor)

time: 74.8 us -> 74.8 us (level)
  no operation moved by 1% of the time
where the time goes in v5:
time: 74.8 us; the launch traced here: 74.7 us
  Pallas kernels  74 us (99%)
    pallas_call x1, Pallas kernels, per_device(): pl.pallas_call(kernel, out_shape=tuple((pltpu.VMEM(*o) for o in outs)), i...  72.1 us
    pallas_call x1, Pallas kernels, per_device(): pl.pallas_call(write_out, out_shape=tuple((jax.ShapeDtypeStruct(*o) for o...  1.9 us

profile of v5, /device:TPU:20, one launch (start us, length us, event | category | flops | bytes accessed | tf_op | source)
XLA Modules:
  0.0 74.7 jit_solution(14874370607240730648)
XLA Ops:
  0.6 72.1 %swiglu_bwd.1 = (bf16[256,256]{1,0:T(8,128)(2,1)S(1)}, f32[256,1792]{1,0:T(8,128)S(1)}, f32[256,1792]{1,0:T(8,128)S(1)}) custom-call(bf16[256,256]{1,0:T(8,128)(2,1)} %inputs.1, bf16[64,1792]{1,0:T(8,128)(2,1)} %gate_pre.1, bf16[64,1792]{1,0:T(8,128)(2,1)} %up_pre.1, bf16[64,1792]{1,0:T(8,128)(2,1)} %hidden_grad.1, bf16[256,1792]{1,0:T(8,128)(2,1)} %gate_weight.1, ...), custom_call_target="tpu_custom_call" | custom-call | flops 7516192768 | bytes 8388608 | tf_op jit(solution)/shard_map/swiglu_bwd/pallas_call | solution.py:408
  72.8 1.9 %write_out.1 = (bf16[256,256]{1,0:T(8,128)(2,1)}, f32[256,1792]{1,0:T(8,128)}, f32[256,1792]{1,0:T(8,128)}) custom-call(bf16[256,256]{1,0:T(8,128)(2,1)S(1)} %get-tuple-element.6.refs_0_, f32[256,1792]{1,0:T(8,128)S(1)} %get-tuple-element.7.refs_1_, f32[256,1792]{1,0:T(8,128)S(1)} %get-tuple-element.8.refs_2_), custom_call_target="tpu_custom_call" | custom-call | tf_op jit(solution)/shard_map/write_out/pallas_call | solution.py:441

commit v6 on v4

--- a/solution.py
+++ b/solution.py
@@ -142,7 +142,9 @@
         kind, far = STREAM[stream]
         for way in (0, 1):
             z_copy(way, stream, hop).wait_recv()
-        if kind == GATE:
+            if kind == GATE and hop < 2:
+                go(z_copy(way, stream, hop + 1))
+        if kind == GATE and hop == 2:
             forward(stream, hop)
         for off in (-(hop + 1), hop + 1):
             if kind == GATE:

time: 74.8 us -> 74.8 us (level)
  no operation moved by 1% of the time
where the time goes in v6:
time: 74.8 us; the launch traced here: 74.7 us
  Pallas kernels  74 us (99%)
    pallas_call x1, Pallas kernels, per_device(): pl.pallas_call(kernel, out_shape=tuple((pltpu.VMEM(*o) for o in outs)), i...  72.1 us
    pallas_call x1, Pallas kernels, per_device(): pl.pallas_call(write_out, out_shape=tuple((jax.ShapeDtypeStruct(*o) for o...  1.9 us

profile of v6, /device:TPU:20, one launch (start us, length us, event | category | flops | bytes accessed | tf_op | source)
XLA Modules:
  0.0 74.7 jit_solution(685840086832131560)
XLA Ops:
  0.6 72.1 %swiglu_bwd.1 = (bf16[256,256]{1,0:T(8,128)(2,1)S(1)}, f32[256,1792]{1,0:T(8,128)S(1)}, f32[256,1792]{1,0:T(8,128)S(1)}) custom-call(bf16[256,256]{1,0:T(8,128)(2,1)} %inputs.1, bf16[64,1792]{1,0:T(8,128)(2,1)} %gate_pre.1, bf16[64,1792]{1,0:T(8,128)(2,1)} %up_pre.1, bf16[64,1792]{1,0:T(8,128)(2,1)} %hidden_grad.1, bf16[256,1792]{1,0:T(8,128)(2,1)} %gate_weight.1, ...), custom_call_target="tpu_custom_call" | custom-call | flops 7516192768 | bytes 8388608 | tf_op jit(solution)/shard_map/swiglu_bwd/pallas_call | solution.py:410
  72.8 1.9 %write_out.1 = (bf16[256,256]{1,0:T(8,128)(2,1)}, f32[256,1792]{1,0:T(8,128)}, f32[256,1792]{1,0:T(8,128)}) custom-call(bf16[256,256]{1,0:T(8,128)(2,1)S(1)} %get-tuple-element.6.refs_0_, f32[256,1792]{1,0:T(8,128)S(1)} %get-tuple-element.7.refs_1_, f32[256,1792]{1,0:T(8,128)S(1)} %get-tuple-element.8.refs_2_), custom_call_target="tpu_custom_call" | custom-call | tf_op jit(solution)/shard_map/write_out/pallas_call | solution.py:443
